TPU v7x, 32 devices: a whole 2x2x4 slice. The times are simulated.
32 devices in a mesh: region: 4 (over z), pos: 8 (over y, x, core).
Axes of the slice: x: 2, y: 2, z: 4, core: 2. Of those that a mesh axis runs over, the one named last changes fastest.
Arguments:
- object_tiles: bfloat16 [2, 512, 1024], P(None, 'region', 'pos'), may hold values from -4.1875 to 4.1875
- probe: float32 [2, 4, 128, 128], replicated, may hold values from -3 to 3
- amplitudes: float32 [4, 32, 128, 128], P('region', 'pos'), may hold values from 0.3 to 6
- offsets: int32 [4, 2, 32], P('region', None, 'pos'), may hold values from 0 to 127
- counts: int32 [4, 8], P('region', 'pos'), may hold values from 1 to 4
Outputs:
- object_grad: float32 [2, 512, 1024], P(None, 'region', 'pos')
- probe_grad: float32 [2, 4, 128, 128], replicated
All inputs are finite; a program needn't handle non-finite values.
Results may differ from a plain program's by a relative error of at most 0.0003.
Values may be sent and summed in bfloat16 or wider, within the bound.
No kernel may reach another device: no remote copies, remote signals or barrier semaphores. Data moves between devices by JAX's collectives and lax.ppermute only.
A program may use at most 64 MiB of HBM per device.

v0:
```python
import functools
import math

import jax
import jax.numpy as jnp
import numpy as np
from jax import lax
from jax.experimental import pallas as pl
from jax.experimental.pallas import tpu as pltpu
from jax.sharding import PartitionSpec as P


def dft_tables(order):
    index = np.arange(order)
    angle = (index[:, None] * index[None, :] % order) * (2.0 * math.pi / order)
    tables = np.stack([np.cos(angle), np.sin(angle)]) / math.sqrt(order)
    return tables.astype(np.float32)


def split(value):
    high = value.astype(jnp.bfloat16)
    low = (value - high.astype(jnp.float32)).astype(jnp.bfloat16)
    return high, low


def dot(a, b):
    return jnp.dot(a, b, preferred_element_type=jnp.float32)


def times_table(value, table_high, table_low):
    rows = table_high.shape[0]
    sums = []
    for start in range(0, value.shape[0], rows):
        high, low = split(value[start : start + rows])
        both = dot(jnp.concatenate([high, low], axis=0), table_high)
        sums.append(both[:rows] + (both[rows:] + dot(high, table_low)))
    return jnp.concatenate(sums, axis=0)


def table_times(tables, value):
    rows = tables.shape[0] // 2
    sums = []
    for start in range(0, value.shape[1], rows):
        high, low = split(value[:, start : start + rows])
        both = dot(tables, high)
        sums.append(both[:rows] + (both[rows:] + dot(tables[:rows], low)))
    return jnp.concatenate(sums, axis=1)


def slots_kernel(
    scale, modes, slot_total, edge, offsets, counts, place, probes, held, own, below, right, other_diag, diag, other_below,
    own_grad, right_grad, lower_grads, keep, send,
    tables, field_left, field_right, grad_left, grad_right, probe_sum, corners, live, semaphores,
):
    scalars = (
        pltpu.make_async_copy(offsets, corners, semaphores.at[0]),
        pltpu.make_async_copy(counts, live, semaphores.at[1]),
    )
    for copy in scalars:
        copy.start()

    def probe(part, mode):
        return probes[part, mode]

    amplitude_rows = 0
    table_rows = amplitude_rows + slot_total * edge // 2
    cos_high, cos_low = split(held[0, pl.ds(table_rows, edge), :])
    sin_high, sin_low = split(held[1, pl.ds(table_rows, edge), :])
    spread_high, spread_low, turn_high, turn_low = (tables.at[k] for k in range(4))
    for spread, turn, cos_part, sin_part in (
        (spread_high, turn_high, cos_high, sin_high),
        (spread_low, turn_low, cos_low, sin_low),
    ):
        for target, upper, lower in ((spread, -sin_part, sin_part), (turn, sin_part, -sin_part)):
            target[:edge, :edge] = cos_part
            target[:edge, edge:] = upper
            target[edge:, :edge] = lower
            target[edge:, edge:] = cos_part
    turn_both = jnp.concatenate([turn_high[...], turn_low[...]], axis=0)
    spread_both = jnp.concatenate([spread_high[...], spread_low[...]], axis=0)
    has_below, has_right, odd_row = place[2] > 0, place[3] > 0, place[4] > 0
    has_diag = jnp.logical_and(has_below, has_right)

    def present(flag, value):
        return jnp.where(flag, value, jnp.zeros_like(value))

    def arrived(flag, first, second):
        return present(flag, jnp.where(odd_row, second[...], first[...]).astype(jnp.float32))

    field_left[:, :edge] = own[...].astype(jnp.float32)
    field_left[:, edge:] = arrived(has_below, below, other_below)
    field_right[:, :edge] = present(has_right, right[...].astype(jnp.float32))
    field_right[:, edge:] = arrived(has_diag, diag, other_diag)
    grad_left[...] = jnp.zeros_like(grad_left)
    grad_right[...] = jnp.zeros_like(grad_right)
    lane = lax.broadcasted_iota(jnp.int32, (edge, edge), 1)
    for copy in scalars:
        copy.wait()
    slots = range(slot_total)
    corner = [(corners[0, 0, slot], corners[0, 1, slot]) for slot in slots]
    in_left = [lane >= col0 for _, col0 in corner]
    crops, halves = [], []
    for slot in slots:
        row0, col0 = corner[slot]
        rows, shift = pl.ds(row0, edge), lax.rem(edge - col0, edge)
        crop_r, crop_i = (
            pltpu.roll(
                jnp.where(in_left[slot], field_left[part, rows, :], field_right[part, rows, :]), shift, 1
            )
            for part in range(2)
        )
        exits = [
            jnp.concatenate(
                [
                    probe(0, m) * crop_r - probe(1, m) * crop_i,
                    probe(0, m) * crop_i + probe(1, m) * crop_r,
                ],
                axis=1,
            )
            for m in range(modes)
        ]
        crops.append((crop_r, crop_i))
        halves.append(times_table(jnp.concatenate(exits, axis=0), spread_high[...], spread_low[...]))
    fars = []
    for half in halves:
        parts = [
            [half[m * edge : (m + 1) * edge, part * edge : (part + 1) * edge] for m in range(modes)]
            for part in range(2)
        ]
        half = jnp.concatenate([jnp.concatenate(part, axis=1) for part in parts], axis=0)
        fars.append(table_times(turn_both, half))
    halves = []
    for slot in slots:
        far = fars[slot]
        squares = far * far
        squares = squares[:edge] + squares[edge:]
        intensity = functools.reduce(
            jnp.add, [squares[:, m * edge : (m + 1) * edge] for m in range(modes)]
        )
        weight = (slot < live[0, 0]).astype(jnp.float32)
        half_slots = slot_total // 2
        amplitude = held[slot // half_slots, pl.ds(amplitude_rows + slot % half_slots * edge, edge), :]
        factor = weight * (1.0 - amplitude * lax.rsqrt(intensity + 1.0))
        factor = jnp.concatenate([factor] * modes, axis=1)
        residual = far * jnp.concatenate([factor, factor], axis=0)
        halves.append(table_times(spread_both, residual))
    backs = []
    for half in halves:
        parts = [
            [half[part * edge : (part + 1) * edge, m * edge : (m + 1) * edge] for part in range(2)]
            for m in range(modes)
        ]
        half = jnp.concatenate([jnp.concatenate(part, axis=1) for part in parts], axis=0)
        backs.append(times_table(half, turn_high[...], turn_low[...]))
    for slot in slots:
        crop_r, crop_i = crops[slot]
        row0, col0 = corner[slot]
        rows = pl.ds(row0, edge)
        object_r = jnp.zeros((edge, edge), jnp.float32)
        object_i = jnp.zeros((edge, edge), jnp.float32)
        for m in range(modes):
            back_r = backs[slot][m * edge : (m + 1) * edge, :edge]
            back_i = backs[slot][m * edge : (m + 1) * edge, edge:]
            object_r += probe(0, m) * back_r + probe(1, m) * back_i
            object_i += probe(0, m) * back_i - probe(1, m) * back_r
            term_r = crop_r * back_r + crop_i * back_i
            term_i = crop_r * back_i - crop_i * back_r
            if slot == 0:
                probe_sum[0, m] = term_r
                probe_sum[1, m] = term_i
            else:
                probe_sum[0, m] += term_r
                probe_sum[1, m] += term_i
        for part, term in enumerate((object_r, object_i)):
            term = pltpu.roll(term, col0, 1)
            grad_left[part, rows, :] += jnp.where(in_left[slot], term, 0.0)
            grad_right[part, rows, :] += jnp.where(in_left[slot], 0.0, term)
    own_grad[...] = grad_left[:, :edge]
    right_grad[...] = present(has_right, grad_right[:, :edge])
    lower_grads[0] = present(has_below, grad_left[:, edge:])
    lower_grads[1] = present(has_diag, grad_right[:, edge:])
    flat = probe_sum.reshape(2 * modes * edge, edge)
    pieces, depth = keep.shape[0], keep.shape[1]
    for target, half in ((keep, place[0]), (send, 1 - place[0])):
        for position in range(pieces):
            chunk = half * pieces + jnp.bitwise_xor(place[1], position)
            rows = pl.ds(pl.multiple_of(chunk * depth, depth), depth)
            target[position] = flat[rows, :] * scale


def on_device(object_tiles, probe, amplitudes, offsets, counts):
    modes, edge = probe.shape[1], probe.shape[2]
    slot_total = amplitudes.shape[1]
    n_region, n_pos = lax.axis_size("region"), lax.axis_size("pos")
    total = n_region * n_pos
    axes = ("region", "pos")
    f32 = jnp.float32

    row_index, column_index = lax.axis_index("region"), lax.axis_index("pos")

    def shifted(block, down, across):
        route = [
            (i * n_pos + j, (i + down) % n_region * n_pos + (j + across) % n_pos)
            for i in range(n_region)
            for j in range(n_pos)
        ]
        return lax.ppermute(block, axes, route)

    pieces = n_pos // 2

    def partner(block, mask):
        return lax.ppermute(block, axes, [(i, i ^ mask) for i in range(total)])

    place = jnp.stack(
        [
            column_index & 1,
            column_index >> 1,
            (row_index < n_region - 1).astype(jnp.int32),
            (column_index < n_pos - 1).astype(jnp.int32),
            row_index & 1,
        ]
    )

    def swapped(first, across):
        route = []
        for i in range(n_region):
            a = i + 1 if (i - first) % 2 == 0 else i - 1
            for j in range(n_pos):
                if 0 <= a < n_region:
                    target = a * n_pos + (j + across) % n_pos
                else:
                    target = i * n_pos + ((j + across) % n_pos if across else j ^ 1)
                route.append((i * n_pos + j, target))
        return lax.ppermute(object_tiles, axes, route)

    right = shifted(object_tiles, 0, -1)
    halo = (swapped(0, 0), right, swapped(1, -1), swapped(0, -1), swapped(1, 0))

    lines = 2 * modes * edge
    smem = pl.BlockSpec(memory_space=pltpu.SMEM)
    vmem = pl.BlockSpec(memory_space=pltpu.VMEM)
    held = jnp.concatenate(
        [
            amplitudes.reshape(2, -1, edge),
            jnp.asarray(dft_tables(edge)),
        ],
        axis=1,
    )
    quadrant = jax.ShapeDtypeStruct((2, edge, edge), f32)
    part = jax.ShapeDtypeStruct((pieces, lines // n_pos, edge), f32)
    scale = 1.0 / math.sqrt(total * slot_total)
    own_grad, right_grad, lower_grads, keep, send = pl.pallas_call(
        functools.partial(slots_kernel, scale, modes, slot_total, edge),
        out_shape=(quadrant, quadrant, jax.ShapeDtypeStruct((2, 2, edge, edge), f32), part, part),
        in_specs=[pl.BlockSpec(memory_space=pl.ANY)] * 2 + [smem] + [vmem] * 8,
        out_specs=(vmem,) * 5,
        scratch_shapes=[pltpu.VMEM((4, 2 * edge, 2 * edge), jnp.bfloat16)]
        + [pltpu.VMEM((2, 2 * edge, edge), f32)] * 4
        + [
            pltpu.VMEM((2, modes, edge, edge), f32),
            pltpu.SMEM(offsets.shape, jnp.int32),
            pltpu.SMEM(counts.shape, jnp.int32),
            pltpu.SemaphoreType.DMA((2,)),
        ],
        compiler_params=pltpu.CompilerParams(vmem_limit_bytes=16 * 1024 * 1024),
    )(offsets, counts, place, probe, held, object_tiles, *halo)

    half = keep + partner(send, 1)
    above = shifted(lower_grads, 1, 0)
    got = [partner(half[k], 2 * k) for k in range(1, pieces)]
    got[-1], above = lax.optimization_barrier((got[-1], above))
    chunk = functools.reduce(jnp.add, got, half[0])
    terms = [partner(chunk, n_pos * k) for k in range(n_region - 1, 0, -1)] + [chunk]
    left = shifted(right_grad + above[1], 0, 1)
    while len(terms) > 1:
        terms = [terms[k] + terms[k + 1] for k in range(0, len(terms), 2)]
    chunk = terms[0]
    gathered = [chunk] + [partner(chunk, 2 * k) for k in range(1, pieces)]
    gathered[-1], left = lax.optimization_barrier((gathered[-1], left))
    forwarded = [partner(piece, 1) for piece in gathered]
    object_grad = own_grad + above[0] + left

    def in_order(parts, index):
        while len(parts) > 1:
            swap, index = index % 2 == 1, index // 2
            parts = [
                jnp.where(swap, jnp.concatenate([b, a], axis=0), jnp.concatenate([a, b], axis=0))
                for a, b in zip(parts[::2], parts[1::2])
            ]
            parts = list(lax.optimization_barrier(tuple(parts)))
        return parts[0]

    halves = [in_order(gathered, column_index // 2), in_order(forwarded, column_index // 2)]
    probe_grad = in_order(halves, column_index % 2)
    return (object_grad, probe_grad.reshape(probe.shape))


def solution(mesh):
    return jax.shard_map(
        on_device,
        mesh=mesh,
        in_specs=(
            P(None, "region", "pos"),
            P(),
            P("region", "pos", None, None),
            P("region", None, "pos"),
            P("region", "pos"),
        ),
        out_specs=(P(None, "region", "pos"), P()),
        check_vma=False,
    )
```

profile of v0, /device:TPU:0, one launch (start us, length us, event | category | flops | bytes accessed | tf_op | source)
XLA Modules:
  0.0 44.5 jit_solution(10501928727544285743)
XLA Ops:
  0.6 0.0 copy-start
  0.6 3.1 %collective-permute-start = (bf16[2,128,128]{2,1,0:T(8,128)(2,1)}, bf16[2,128,128]{2,1,0:T(8,128)(2,1)S(1)}, u32[]{:S(2)}, u32[]{:S(2)}) collective-permute-start(bf16[2,128,128]{2,1,0:T(8,128)(2,1)} %own.1), channel_id=1, source_target_pairs={{0,8},{1,9},{2,10},{3,11},{4,12},{5,13},{6,14},{7,15},{8,0},{9,1},... | collective-permute-start | bytes 196616 | tf_op jit(solution)/shard_map/ppermute | solution.py:234
  3.7 1.6 %collective-permute-start.1 = (bf16[2,128,128]{2,1,0:T(8,128)(2,1)}, bf16[2,128,128]{2,1,0:T(8,128)(2,1)S(1)}, u32[]{:S(2)}, u32[]{:S(2)}) collective-permute-start(bf16[2,128,128]{2,1,0:T(8,128)(2,1)} %own.1), channel_id=1, source_target_pairs={{0,7},{1,0},{2,1},{3,2},{4,3},{5,4},{6,5},{7,6},{8,15},{9,8},{10,9... | collective-permute-start | bytes 196616 | tf_op jit(solution)/shard_map/ppermute | solution.py:207
  5.3 1.0 %collective-permute-start.2 = (bf16[2,128,128]{2,1,0:T(8,128)(2,1)}, bf16[2,128,128]{2,1,0:T(8,128)(2,1)S(1)}, u32[]{:S(2)}, u32[]{:S(2)}) collective-permute-start(bf16[2,128,128]{2,1,0:T(8,128)(2,1)} %own.1), channel_id=1, source_target_pairs={{0,7},{1,0},{2,1},{3,2},{4,3},{5,4},{6,5},{7,6},{8,23},{9,16},{10,... | collective-permute-start | bytes 196616 | tf_op jit(solution)/shard_map/ppermute | solution.py:234
  6.3 2.2 %collective-permute-start.3 = (bf16[2,128,128]{2,1,0:T(8,128)(2,1)}, bf16[2,128,128]{2,1,0:T(8,128)(2,1)S(1)}, u32[]{:S(2)}, u32[]{:S(2)}) collective-permute-start(bf16[2,128,128]{2,1,0:T(8,128)(2,1)} %own.1), channel_id=1, source_target_pairs={{0,15},{1,8},{2,9},{3,10},{4,11},{5,12},{6,13},{7,14},{8,7},{9,0},... | collective-permute-start | bytes 196616 | tf_op jit(solution)/shard_map/ppermute | solution.py:234
  8.5 0.5 %collective-permute-start.4 = (bf16[2,128,128]{2,1,0:T(8,128)(2,1)}, bf16[2,128,128]{2,1,0:T(8,128)(2,1)S(1)}, u32[]{:S(2)}, u32[]{:S(2)}) collective-permute-start(bf16[2,128,128]{2,1,0:T(8,128)(2,1)} %own.1), channel_id=1, source_target_pairs={{0,1},{1,0},{2,3},{3,2},{4,5},{5,4},{6,7},{7,6},{8,16},{9,17},{10,... | collective-permute-start | bytes 196616 | tf_op jit(solution)/shard_map/ppermute | solution.py:234
  9.6 0.1 stack.31.place
  9.7 0.0 copy-start.1
  9.7 0.0 copy-start.2
  9.7 1.1 %pad_maximum_fusion.held = f32[2,384,128]{2,1,0:T(8,128)S(1)} fusion(f32[2,128,128]{2,1,0:T(8,128)} %constant.66.clone, f32[2,256,128]{2,1,0:T(8,128)} %bitcast.28), kind=kLoop, calls=%fused_computation.1 | loop fusion | flops 98304 | bytes 786432 | tf_op jit(solution)/shard_map/concatenate | solution.py:242
  10.8 0.0 collective-permute-done.below
  10.8 0.0 collective-permute-done.1.right
  10.8 0.0 collective-permute-done.2.other_diag
  10.8 0.3 collective-permute-done.3.diag
  11.1 0.0 collective-permute-done.4.other_below
  11.1 0.0 copy-done
  11.1 0.0 copy-done.1
  11.1 0.0 copy-done.2
  11.1 5.0 %shard_map.77 = (f32[2,128,128]{2,1,0:T(8,128)S(1)}, f32[2,128,128]{2,1,0:T(8,128)S(1)}, f32[2,2,128,128]{3,2,1,0:T(8,128)S(1)}, f32[4,128,128]{2,1,0:T(8,128)S(1)}, f32[4,128,128]{2,1,0:T(8,128)S(1)}) custom-call(s32[1,2,4]{2,1,0:T(2,128)S(1)} %copy-done.2, s32[1,1]{1,0:T(1,128)S(6)} %copy.8.counts, s32[5]{0:T(128)S(1)} %stack.31.place, ...), custom_call_target="tpu_custom_call" | custom-call | tf_op jit(solution)/shard_map/pallas_call | solution.py:252
  16.2 0.1 collective-permute-start.5
  16.3 2.3 %collective-permute-start.7 = (f32[2,2,128,128]{3,2,1,0:T(8,128)S(1)}, f32[2,2,128,128]{3,2,1,0:T(8,128)S(1)}, u32[]{:S(2)}, u32[]{:S(2)}) collective-permute-start(f32[2,2,128,128]{3,2,1,0:T(8,128)S(1)} %get-tuple-element.18), channel_id=1, source_target_pairs={{0,8},{1,9},{2,10},{3,11},{4,12},{5,13},{6,14},{7,15},{8,16},{9,17... | collective-permute-start | bytes 786440 | tf_op jit(solution)/shard_map/ppermute | solution.py:207
  18.6 0.0 collective-permute-done.5
  18.6 2.3 %collective-permute-start.6 = (f32[128,128]{1,0:T(8,128)S(1)}, f32[128,128]{1,0:T(8,128)S(1)}, u32[]{:S(2)}, u32[]{:S(2)}) collective-permute-start(f32[128,128]{1,0:T(8,128)S(1)} %get-tuple-element.30), channel_id=1, source_target_pairs={{0,6},{1,7},{2,4},{3,5},{4,2},{5,3},{6,0},{7,1},{8,14},{9,15},{10,... | collective-permute-start | bytes 196616 | tf_op jit(solution)/shard_map/ppermute | solution.py:212
  21.0 0.0 collective-permute-start.8
  21.0 1.2 %collective-permute-start.9 = (f32[128,128]{1,0:T(8,128)S(1)}, f32[128,128]{1,0:T(8,128)S(1)}, u32[]{:S(2)}, u32[]{:S(2)}) collective-permute-start(f32[128,128]{1,0:T(8,128)S(1)} %get-tuple-element.29), channel_id=1, source_target_pairs={{0,4},{1,5},{2,6},{3,7},{4,0},{5,1},{6,2},{7,3},{8,12},{9,13},{10,... | collective-permute-start | bytes 196616 | tf_op jit(solution)/shard_map/ppermute | solution.py:212
  22.2 4.6 %collective-permute-done.7 = f32[2,2,128,128]{3,2,1,0:T(8,128)S(1)} collective-permute-done((f32[2,2,128,128]{3,2,1,0:T(8,128)S(1)}, f32[2,2,128,128]{3,2,1,0:T(8,128)S(1)}, u32[]{:S(2)}, u32[]{:S(2)}) %collective-permute-start.7) | collective-permute-done | bytes 262176 | tf_op jit(solution)/shard_map/ppermute | solution.py:207
  26.8 0.0 collective-permute-done.6
  26.8 0.0 collective-permute-done.8
  26.8 0.0 collective-permute-done.9
  26.8 1.1 %collective-permute-start.10 = (f32[128,128]{1,0:T(8,128)S(1)}, f32[128,128]{1,0:T(8,128)S(1)}, u32[]{:S(2)}, u32[]{:S(2)}) collective-permute-start(f32[128,128]{1,0:T(8,128)S(1)} %fusion.3), channel_id=1, source_target_pairs={{0,24},{1,25},{2,26},{3,27},{4,28},{5,29},{6,30},{7,31},{8,16},{9,... | collective-permute-start | bytes 196616 | tf_op jit(solution)/shard_map/ppermute | solution.py:212
  27.9 0.9 %collective-permute-start.11 = (f32[128,128]{1,0:T(8,128)S(1)}, f32[128,128]{1,0:T(8,128)S(1)}, u32[]{:S(2)}, u32[]{:S(2)}) collective-permute-start(f32[128,128]{1,0:T(8,128)S(1)} %fusion.3), channel_id=1, source_target_pairs={{0,16},{1,17},{2,18},{3,19},{4,20},{5,21},{6,22},{7,23},{8,24},{9,... | collective-permute-start | bytes 196616 | tf_op jit(solution)/shard_map/ppermute | solution.py:212
  28.8 2.5 %collective-permute-start.12 = (f32[128,128]{1,0:T(8,128)S(1)}, f32[128,128]{1,0:T(8,128)S(1)}, u32[]{:S(2)}, u32[]{:S(2)}) collective-permute-start(f32[128,128]{1,0:T(8,128)S(1)} %fusion.3), channel_id=1, source_target_pairs={{0,8},{1,9},{2,10},{3,11},{4,12},{5,13},{6,14},{7,15},{8,0},{9,1},... | collective-permute-start | bytes 196616 | tf_op jit(solution)/shard_map/ppermute | solution.py:212
  31.3 0.1 collective-permute-start.14
  31.3 2.4 %collective-permute-done.10 = f32[128,128]{1,0:T(8,128)S(1)} collective-permute-done((f32[128,128]{1,0:T(8,128)S(1)}, f32[128,128]{1,0:T(8,128)S(1)}, u32[]{:S(2)}, u32[]{:S(2)}) %collective-permute-start.10) | collective-permute-done | bytes 65568 | tf_op jit(solution)/shard_map/ppermute | solution.py:212
  33.8 1.5 %collective-permute-done.11 = f32[128,128]{1,0:T(8,128)S(1)} collective-permute-done((f32[128,128]{1,0:T(8,128)S(1)}, f32[128,128]{1,0:T(8,128)S(1)}, u32[]{:S(2)}, u32[]{:S(2)}) %collective-permute-start.11) | collective-permute-done | bytes 65568 | tf_op jit(solution)/shard_map/ppermute | solution.py:212
  35.2 0.0 collective-permute-done.12
  35.3 1.4 %collective-permute-start.13 = (f32[128,128]{1,0:T(8,128)S(1)}, f32[128,128]{1,0:T(8,128)S(1)}, u32[]{:S(2)}, u32[]{:S(2)}) collective-permute-start(f32[128,128]{1,0:T(8,128)S(1)} %add_add_fusion), channel_id=1, source_target_pairs={{0,6},{1,7},{2,4},{3,5},{4,2},{5,3},{6,0},{7,1},{8,14},{9,15},{10,... | collective-permute-start | bytes 196616 | tf_op jit(solution)/shard_map/ppermute | solution.py:212
  36.7 1.0 %collective-permute-start.19 = (f32[128,128]{1,0:T(8,128)S(1)}, f32[128,128]{1,0:T(8,128)S(1)}, u32[]{:S(2)}, u32[]{:S(2)}) collective-permute-start(f32[128,128]{1,0:T(8,128)S(1)} %add_add_fusion), channel_id=1, source_target_pairs={{0,4},{1,5},{2,6},{3,7},{4,0},{5,1},{6,2},{7,3},{8,12},{9,13},{10,... | collective-permute-start | bytes 196616 | tf_op jit(solution)/shard_map/ppermute | solution.py:212
  37.6 1.2 %collective-permute-start.15 = (f32[128,128]{1,0:T(8,128)S(1)}, f32[128,128]{1,0:T(8,128)S(1)}, u32[]{:S(2)}, u32[]{:S(2)}) collective-permute-start(f32[128,128]{1,0:T(8,128)S(1)} %add_add_fusion), channel_id=1, source_target_pairs={{0,2},{1,3},{2,0},{3,1},{4,6},{5,7},{6,4},{7,5},{8,10},{9,11},{10,... | collective-permute-start | bytes 196616 | tf_op jit(solution)/shard_map/ppermute | solution.py:212
  38.8 0.0 collective-permute-start.17
  38.8 2.2 %collective-permute-done.13 = f32[128,128]{1,0:T(8,128)S(1)} collective-permute-done((f32[128,128]{1,0:T(8,128)S(1)}, f32[128,128]{1,0:T(8,128)S(1)}, u32[]{:S(2)}, u32[]{:S(2)}) %collective-permute-start.13) | collective-permute-done | bytes 65568 | tf_op jit(solution)/shard_map/ppermute | solution.py:212
  41.0 0.0 collective-permute-done.14
  41.0 0.0 collective-permute-start.18
  41.0 0.7 %fusion = f32[2,128,128]{2,1,0:T(8,128)} fusion(f32[2,128,128]{2,1,0:T(8,128)S(1)} %collective-permute-done.14, f32[2,128,128]{2,1,0:T(8,128)S(1)} %get-tuple-element.15, f32[2,2,128,128]{3,2,1,0:T(8,128)S(1)} %collective-permute-done.7), kind=kLoop, calls=%fused_computation.10 | loop fusion | flops 65536 | bytes 524288 | tf_op jit(solution)/shard_map/add | solution.py:281
  41.7 0.0 collective-permute-done.19
  41.7 0.5 %collective-permute-start.20 = (f32[128,128]{1,0:T(8,128)S(1)}, f32[128,128]{1,0:T(8,128)S(1)}, u32[]{:S(2)}, u32[]{:S(2)}) collective-permute-start(f32[128,128]{1,0:T(8,128)S(1)} %collective-permute-done.19), channel_id=1, source_target_pairs={{0,1},{1,0},{2,3},{3,2},{4,5},{5,4},{6,7},{7,6},{8,9},{9,8},{10,11... | collective-permute-start | bytes 196616 | tf_op jit(solution)/shard_map/ppermute | solution.py:212
  42.2 0.0 collective-permute-done.15
  42.2 0.1 collective-permute-start.16
  42.3 0.0 collective-permute-done.18
  42.3 0.8 %collective-permute-done.20 = f32[128,128]{1,0:T(8,128)S(1)} collective-permute-done((f32[128,128]{1,0:T(8,128)S(1)}, f32[128,128]{1,0:T(8,128)S(1)}, u32[]{:S(2)}, u32[]{:S(2)}) %collective-permute-start.20) | collective-permute-done | bytes 65568 | tf_op jit(solution)/shard_map/ppermute | solution.py:212
  43.1 0.0 collective-permute-done.17
  43.1 0.4 collective-permute-done.16
  43.6 0.8 %maximum_select_fusion = f32[1024,128]{1,0:T(8,128)} fusion(f32[512,128]{1,0:T(8,128)S(1)} %get-tuple-element.32, f32[512,128]{1,0:T(8,128)S(1)} %get-tuple-element.31, pred[]{:T(512)S(6)} %eq.18), kind=kLoop, calls=%fused_computation | loop fusion | flops 393216 | bytes 1048577 | tf_op jit(solution)/shard_map/jit(_where)/select_n | solution.py:287
  (10 shorter events, 0.2 us)
Async XLA Ops:
  0.6 10.5 %copy-start = (f32[2,4,128,128]{3,2,1,0:T(8,128)S(1)}, f32[2,4,128,128]{3,2,1,0:T(8,128)}, u32[]{:S(2)}) copy-start(f32[2,4,128,128]{3,2,1,0:T(8,128)} %probes.1) | copy-start | bytes 1572868
  0.6 10.2 %collective-permute-start = (bf16[2,128,128]{2,1,0:T(8,128)(2,1)}, bf16[2,128,128]{2,1,0:T(8,128)(2,1)S(1)}, u32[]{:S(2)}, u32[]{:S(2)}) collective-permute-start(bf16[2,128,128]{2,1,0:T(8,128)(2,1)} %own.1), channel_id=1, source_target_pairs={{0,8},{1,9},{2,10},{3,11},{4,12},{5,13},{6,14},{7,15},{8,0},{9,1},... | collective-permute-start | bytes 196616 | tf_op jit(solution)/shard_map/ppermute | solution.py:234
  3.7 7.1 %collective-permute-start.1 = (bf16[2,128,128]{2,1,0:T(8,128)(2,1)}, bf16[2,128,128]{2,1,0:T(8,128)(2,1)S(1)}, u32[]{:S(2)}, u32[]{:S(2)}) collective-permute-start(bf16[2,128,128]{2,1,0:T(8,128)(2,1)} %own.1), channel_id=1, source_target_pairs={{0,7},{1,0},{2,1},{3,2},{4,3},{5,4},{6,5},{7,6},{8,15},{9,8},{10,9... | collective-permute-start | bytes 196616 | tf_op jit(solution)/shard_map/ppermute | solution.py:207
  5.3 5.5 %collective-permute-start.2 = (bf16[2,128,128]{2,1,0:T(8,128)(2,1)}, bf16[2,128,128]{2,1,0:T(8,128)(2,1)S(1)}, u32[]{:S(2)}, u32[]{:S(2)}) collective-permute-start(bf16[2,128,128]{2,1,0:T(8,128)(2,1)} %own.1), channel_id=1, source_target_pairs={{0,7},{1,0},{2,1},{3,2},{4,3},{5,4},{6,5},{7,6},{8,23},{9,16},{10,... | collective-permute-start | bytes 196616 | tf_op jit(solution)/shard_map/ppermute | solution.py:234
  6.3 4.8 %collective-permute-start.3 = (bf16[2,128,128]{2,1,0:T(8,128)(2,1)}, bf16[2,128,128]{2,1,0:T(8,128)(2,1)S(1)}, u32[]{:S(2)}, u32[]{:S(2)}) collective-permute-start(bf16[2,128,128]{2,1,0:T(8,128)(2,1)} %own.1), channel_id=1, source_target_pairs={{0,15},{1,8},{2,9},{3,10},{4,11},{5,12},{6,13},{7,14},{8,7},{9,0},... | collective-permute-start | bytes 196616 | tf_op jit(solution)/shard_map/ppermute | solution.py:234
  8.5 2.6 %collective-permute-start.4 = (bf16[2,128,128]{2,1,0:T(8,128)(2,1)}, bf16[2,128,128]{2,1,0:T(8,128)(2,1)S(1)}, u32[]{:S(2)}, u32[]{:S(2)}) collective-permute-start(bf16[2,128,128]{2,1,0:T(8,128)(2,1)} %own.1), channel_id=1, source_target_pairs={{0,1},{1,0},{2,3},{3,2},{4,5},{5,4},{6,7},{7,6},{8,16},{9,17},{10,... | collective-permute-start | bytes 196616 | tf_op jit(solution)/shard_map/ppermute | solution.py:234
  9.7 1.4 %copy-start.1 = (bf16[2,128,128]{2,1,0:T(8,128)(2,1)S(1)}, bf16[2,128,128]{2,1,0:T(8,128)(2,1)}, u32[]{:S(2)}) copy-start(bf16[2,128,128]{2,1,0:T(8,128)(2,1)} %own.1) | copy-start | bytes 196612
  9.7 1.4 %copy-start.2 = (s32[1,2,4]{2,1,0:T(2,128)S(1)}, s32[1,2,4]{2,1,0:T(2,128)}, u32[]{:S(2)}) copy-start(s32[1,2,4]{2,1,0:T(2,128)} %offsets.1) | copy-start | bytes 100
  16.2 2.4 %collective-permute-start.5 = (f32[4,128,128]{2,1,0:T(8,128)S(1)}, f32[4,128,128]{2,1,0:T(8,128)S(1)}, u32[]{:S(2)}, u32[]{:S(2)}) collective-permute-start(f32[4,128,128]{2,1,0:T(8,128)S(1)} %get-tuple-element.17), channel_id=1, source_target_pairs={{0,1},{1,0},{2,3},{3,2},{4,5},{5,4},{6,7},{7,6},{8,9},{9,8},{10,11... | collective-permute-start | bytes 786440 | tf_op jit(solution)/shard_map/ppermute | solution.py:212
  16.3 10.5 %collective-permute-start.7 = (f32[2,2,128,128]{3,2,1,0:T(8,128)S(1)}, f32[2,2,128,128]{3,2,1,0:T(8,128)S(1)}, u32[]{:S(2)}, u32[]{:S(2)}) collective-permute-start(f32[2,2,128,128]{3,2,1,0:T(8,128)S(1)} %get-tuple-element.18), channel_id=1, source_target_pairs={{0,8},{1,9},{2,10},{3,11},{4,12},{5,13},{6,14},{7,15},{8,16},{9,17... | collective-permute-start | bytes 786440 | tf_op jit(solution)/shard_map/ppermute | solution.py:207
  18.6 8.1 %collective-permute-start.6 = (f32[128,128]{1,0:T(8,128)S(1)}, f32[128,128]{1,0:T(8,128)S(1)}, u32[]{:S(2)}, u32[]{:S(2)}) collective-permute-start(f32[128,128]{1,0:T(8,128)S(1)} %get-tuple-element.30), channel_id=1, source_target_pairs={{0,6},{1,7},{2,4},{3,5},{4,2},{5,3},{6,0},{7,1},{8,14},{9,15},{10,... | collective-permute-start | bytes 196616 | tf_op jit(solution)/shard_map/ppermute | solution.py:212
  21.0 5.8 %collective-permute-start.8 = (f32[128,128]{1,0:T(8,128)S(1)}, f32[128,128]{1,0:T(8,128)S(1)}, u32[]{:S(2)}, u32[]{:S(2)}) collective-permute-start(f32[128,128]{1,0:T(8,128)S(1)} %get-tuple-element.28), channel_id=1, source_target_pairs={{0,2},{1,3},{2,0},{3,1},{4,6},{5,7},{6,4},{7,5},{8,10},{9,11},{10,... | collective-permute-start | bytes 196616 | tf_op jit(solution)/shard_map/ppermute | solution.py:212
  21.0 5.8 %collective-permute-start.9 = (f32[128,128]{1,0:T(8,128)S(1)}, f32[128,128]{1,0:T(8,128)S(1)}, u32[]{:S(2)}, u32[]{:S(2)}) collective-permute-start(f32[128,128]{1,0:T(8,128)S(1)} %get-tuple-element.29), channel_id=1, source_target_pairs={{0,4},{1,5},{2,6},{3,7},{4,0},{5,1},{6,2},{7,3},{8,12},{9,13},{10,... | collective-permute-start | bytes 196616 | tf_op jit(solution)/shard_map/ppermute | solution.py:212
  26.8 7.0 %collective-permute-start.10 = (f32[128,128]{1,0:T(8,128)S(1)}, f32[128,128]{1,0:T(8,128)S(1)}, u32[]{:S(2)}, u32[]{:S(2)}) collective-permute-start(f32[128,128]{1,0:T(8,128)S(1)} %fusion.3), channel_id=1, source_target_pairs={{0,24},{1,25},{2,26},{3,27},{4,28},{5,29},{6,30},{7,31},{8,16},{9,... | collective-permute-start | bytes 196616 | tf_op jit(solution)/shard_map/ppermute | solution.py:212
  27.9 7.4 %collective-permute-start.11 = (f32[128,128]{1,0:T(8,128)S(1)}, f32[128,128]{1,0:T(8,128)S(1)}, u32[]{:S(2)}, u32[]{:S(2)}) collective-permute-start(f32[128,128]{1,0:T(8,128)S(1)} %fusion.3), channel_id=1, source_target_pairs={{0,16},{1,17},{2,18},{3,19},{4,20},{5,21},{6,22},{7,23},{8,24},{9,... | collective-permute-start | bytes 196616 | tf_op jit(solution)/shard_map/ppermute | solution.py:212
  28.8 6.5 %collective-permute-start.12 = (f32[128,128]{1,0:T(8,128)S(1)}, f32[128,128]{1,0:T(8,128)S(1)}, u32[]{:S(2)}, u32[]{:S(2)}) collective-permute-start(f32[128,128]{1,0:T(8,128)S(1)} %fusion.3), channel_id=1, source_target_pairs={{0,8},{1,9},{2,10},{3,11},{4,12},{5,13},{6,14},{7,15},{8,0},{9,1},... | collective-permute-start | bytes 196616 | tf_op jit(solution)/shard_map/ppermute | solution.py:212
  31.3 9.7 %collective-permute-start.14 = (f32[2,128,128]{2,1,0:T(8,128)S(1)}, f32[2,128,128]{2,1,0:T(8,128)S(1)}, u32[]{:S(2)}, u32[]{:S(2)}) collective-permute-start(f32[2,128,128]{2,1,0:T(8,128)S(1)} %bitcast_add_fusion), channel_id=1, source_target_pairs={{0,1},{1,2},{2,3},{3,4},{4,5},{5,6},{6,7},{7,0},{8,9},{9,10},{10,1... | collective-permute-start | bytes 393224 | tf_op jit(solution)/shard_map/ppermute | solution.py:207
  35.3 5.7 %collective-permute-start.13 = (f32[128,128]{1,0:T(8,128)S(1)}, f32[128,128]{1,0:T(8,128)S(1)}, u32[]{:S(2)}, u32[]{:S(2)}) collective-permute-start(f32[128,128]{1,0:T(8,128)S(1)} %add_add_fusion), channel_id=1, source_target_pairs={{0,6},{1,7},{2,4},{3,5},{4,2},{5,3},{6,0},{7,1},{8,14},{9,15},{10,... | collective-permute-start | bytes 196616 | tf_op jit(solution)/shard_map/ppermute | solution.py:212
  36.7 5.0 %collective-permute-start.19 = (f32[128,128]{1,0:T(8,128)S(1)}, f32[128,128]{1,0:T(8,128)S(1)}, u32[]{:S(2)}, u32[]{:S(2)}) collective-permute-start(f32[128,128]{1,0:T(8,128)S(1)} %add_add_fusion), channel_id=1, source_target_pairs={{0,4},{1,5},{2,6},{3,7},{4,0},{5,1},{6,2},{7,3},{8,12},{9,13},{10,... | collective-permute-start | bytes 196616 | tf_op jit(solution)/shard_map/ppermute | solution.py:212
  37.6 4.6 %collective-permute-start.15 = (f32[128,128]{1,0:T(8,128)S(1)}, f32[128,128]{1,0:T(8,128)S(1)}, u32[]{:S(2)}, u32[]{:S(2)}) collective-permute-start(f32[128,128]{1,0:T(8,128)S(1)} %add_add_fusion), channel_id=1, source_target_pairs={{0,2},{1,3},{2,0},{3,1},{4,6},{5,7},{6,4},{7,5},{8,10},{9,11},{10,... | collective-permute-start | bytes 196616 | tf_op jit(solution)/shard_map/ppermute | solution.py:212
  38.8 4.3 %collective-permute-start.17 = (f32[128,128]{1,0:T(8,128)S(1)}, f32[128,128]{1,0:T(8,128)S(1)}, u32[]{:S(2)}, u32[]{:S(2)}) collective-permute-start(f32[128,128]{1,0:T(8,128)S(1)} %add_add_fusion), channel_id=1, source_target_pairs={{0,1},{1,0},{2,3},{3,2},{4,5},{5,4},{6,7},{7,6},{8,9},{9,8},{10,11... | collective-permute-start | bytes 196616 | tf_op jit(solution)/shard_map/ppermute | solution.py:212
  41.0 1.3 %collective-permute-start.18 = (f32[128,128]{1,0:T(8,128)S(1)}, f32[128,128]{1,0:T(8,128)S(1)}, u32[]{:S(2)}, u32[]{:S(2)}) collective-permute-start(f32[128,128]{1,0:T(8,128)S(1)} %collective-permute-done.13), channel_id=1, source_target_pairs={{0,1},{1,0},{2,3},{3,2},{4,5},{5,4},{6,7},{7,6},{8,9},{9,8},{10,11... | collective-permute-start | bytes 196616 | tf_op jit(solution)/shard_map/ppermute | solution.py:212
  41.7 1.4 %collective-permute-start.20 = (f32[128,128]{1,0:T(8,128)S(1)}, f32[128,128]{1,0:T(8,128)S(1)}, u32[]{:S(2)}, u32[]{:S(2)}) collective-permute-start(f32[128,128]{1,0:T(8,128)S(1)} %collective-permute-done.19), channel_id=1, source_target_pairs={{0,1},{1,0},{2,3},{3,2},{4,5},{5,4},{6,7},{7,6},{8,9},{9,8},{10,11... | collective-permute-start | bytes 196616 | tf_op jit(solution)/shard_map/ppermute | solution.py:212
  42.2 1.3 %collective-permute-start.16 = (f32[128,128]{1,0:T(8,128)S(1)}, f32[128,128]{1,0:T(8,128)S(1)}, u32[]{:S(2)}, u32[]{:S(2)}) collective-permute-start(f32[128,128]{1,0:T(8,128)S(1)} %collective-permute-done.15), channel_id=1, source_target_pairs={{0,1},{1,0},{2,3},{3,2},{4,5},{5,4},{6,7},{7,6},{8,9},{9,8},{10,11... | collective-permute-start | bytes 196616 | tf_op jit(solution)/shard_map/ppermute | solution.py:212
where the time goes:
time: 44.6 us; the launch traced here: 44.5 us
  starting transfers between devices  22.9 us (51%)
  waiting for transfers between devices  12.2 us (27%)
  Pallas kernels  5.04 us (11%)
  other arithmetic  2.77 us (6%)
  between operations  1.43 us (3%)
    ppermute x14, starting transfers between devices, partner(): return lax.ppermute(block, axes, [(i, i ^ mask) for i in range(total)])  12.2 us
    ppermute x14, waiting for transfers between devices, partner(): return lax.ppermute(block, axes, [(i, i ^ mask) for i in range(total)])  7.3 us
    ppermute x4, starting transfers between devices, swapped(): return lax.ppermute(object_tiles, axes, route)  6.75 us
    pallas_call x1, Pallas kernels, on_device(): pl.pallas_call(functools.partial(slots_kernel, scale, modes, slot_total,...  5.04 us
    ppermute x3, waiting for transfers between devices, shifted(): return lax.ppermute(block, axes, route)  4.59 us
    ppermute x3, starting transfers between devices, shifted(): return lax.ppermute(block, axes, route)  3.96 us
    concatenate x1, other arithmetic, on_device(): jnp.concatenate([amplitudes.reshape(2, -1, edge), jnp.asarray(dft_tables(...  1.07 us
    select_n x6, other arithmetic, in_order(): jnp.where(swap, jnp.concatenate([b, a], axis=0), jnp.concatenate([a, b],...  0.93 us
  transfers between devices with their start and end apart: 21, of which 7 were waited for; matrix products, arithmetic and copies ran while one was open for 4% of the time, Pallas kernels for 0%

commit v1 on v0

--- a/solution.py
+++ b/solution.py
@@ -270,7 +270,7 @@
     got = [partner(half[k], 2 * k) for k in range(1, pieces)]
     got[-1], above = lax.optimization_barrier((got[-1], above))
     chunk = functools.reduce(jnp.add, got, half[0])
-    terms = [partner(chunk, n_pos * k) for k in range(n_region - 1, 0, -1)] + [chunk]
+    terms = [chunk] + [partner(chunk, n_pos * k) for k in range(1, n_region)]
     left = shifted(right_grad + above[1], 0, 1)
     while len(terms) > 1:
         terms = [terms[k] + terms[k + 1] for k in range(0, len(terms), 2)]

time: 44.6 us -> 44.4 us (level)
  no operation moved by 1% of the time
where the time goes in v1:
time: 44.4 us; the launch traced here: 44.2 us
  starting transfers between devices  22.9 us (52%)
  waiting for transfers between devices  11.9 us (27%)
  Pallas kernels  5.05 us (11%)
  other arithmetic  2.77 us (6%)
  between operations  1.44 us (3%)
    ppermute x14, starting transfers between devices, partner(): return lax.ppermute(block, axes, [(i, i ^ mask) for i in range(total)])  12.2 us
    ppermute x14, waiting for transfers between devices, partner(): return lax.ppermute(block, axes, [(i, i ^ mask) for i in range(total)])  7.06 us
    ppermute x4, starting transfers between devices, swapped(): return lax.ppermute(object_tiles, axes, route)  6.75 us
    pallas_call x1, Pallas kernels, on_device(): pl.pallas_call(functools.partial(slots_kernel, scale, modes, slot_total,...  5.05 us
    ppermute x3, waiting for transfers between devices, shifted(): return lax.ppermute(block, axes, route)  4.59 us
    ppermute x3, starting transfers between devices, shifted(): return lax.ppermute(block, axes, route)  3.96 us
    concatenate x1, other arithmetic, on_device(): jnp.concatenate([amplitudes.reshape(2, -1, edge), jnp.asarray(dft_tables(...  1.07 us
    select_n x6, other arithmetic, in_order(): jnp.where(swap, jnp.concatenate([b, a], axis=0), jnp.concatenate([a, b],...  0.93 us
  transfers between devices with their start and end apart: 21, of which 7 were waited for; matrix products, arithmetic and copies ran while one was open for 4% of the time, Pallas kernels for 0%

profile of v1, /device:TPU:0, one launch (start us, length us, event | category | flops | bytes accessed | tf_op | source)
XLA Modules:
  0.0 44.2 jit_solution(14822421720589443445)
XLA Ops:
  0.6 0.0 copy-start
  0.6 3.1 %collective-permute-start = (bf16[2,128,128]{2,1,0:T(8,128)(2,1)}, bf16[2,128,128]{2,1,0:T(8,128)(2,1)S(1)}, u32[]{:S(2)}, u32[]{:S(2)}) collective-permute-start(bf16[2,128,128]{2,1,0:T(8,128)(2,1)} %own.1), channel_id=1, source_target_pairs={{0,8},{1,9},{2,10},{3,11},{4,12},{5,13},{6,14},{7,15},{8,0},{9,1},... | collective-permute-start | bytes 196616 | tf_op jit(solution)/shard_map/ppermute | solution.py:234
  3.7 1.6 %collective-permute-start.1 = (bf16[2,128,128]{2,1,0:T(8,128)(2,1)}, bf16[2,128,128]{2,1,0:T(8,128)(2,1)S(1)}, u32[]{:S(2)}, u32[]{:S(2)}) collective-permute-start(bf16[2,128,128]{2,1,0:T(8,128)(2,1)} %own.1), channel_id=1, source_target_pairs={{0,7},{1,0},{2,1},{3,2},{4,3},{5,4},{6,5},{7,6},{8,15},{9,8},{10,9... | collective-permute-start | bytes 196616 | tf_op jit(solution)/shard_map/ppermute | solution.py:207
  5.3 1.0 %collective-permute-start.2 = (bf16[2,128,128]{2,1,0:T(8,128)(2,1)}, bf16[2,128,128]{2,1,0:T(8,128)(2,1)S(1)}, u32[]{:S(2)}, u32[]{:S(2)}) collective-permute-start(bf16[2,128,128]{2,1,0:T(8,128)(2,1)} %own.1), channel_id=1, source_target_pairs={{0,7},{1,0},{2,1},{3,2},{4,3},{5,4},{6,5},{7,6},{8,23},{9,16},{10,... | collective-permute-start | bytes 196616 | tf_op jit(solution)/shard_map/ppermute | solution.py:234
  6.3 2.2 %collective-permute-start.3 = (bf16[2,128,128]{2,1,0:T(8,128)(2,1)}, bf16[2,128,128]{2,1,0:T(8,128)(2,1)S(1)}, u32[]{:S(2)}, u32[]{:S(2)}) collective-permute-start(bf16[2,128,128]{2,1,0:T(8,128)(2,1)} %own.1), channel_id=1, source_target_pairs={{0,15},{1,8},{2,9},{3,10},{4,11},{5,12},{6,13},{7,14},{8,7},{9,0},... | collective-permute-start | bytes 196616 | tf_op jit(solution)/shard_map/ppermute | solution.py:234
  8.5 0.5 %collective-permute-start.4 = (bf16[2,128,128]{2,1,0:T(8,128)(2,1)}, bf16[2,128,128]{2,1,0:T(8,128)(2,1)S(1)}, u32[]{:S(2)}, u32[]{:S(2)}) collective-permute-start(bf16[2,128,128]{2,1,0:T(8,128)(2,1)} %own.1), channel_id=1, source_target_pairs={{0,1},{1,0},{2,3},{3,2},{4,5},{5,4},{6,7},{7,6},{8,16},{9,17},{10,... | collective-permute-start | bytes 196616 | tf_op jit(solution)/shard_map/ppermute | solution.py:234
  9.6 0.1 stack.31.place
  9.7 0.0 copy-start.1
  9.7 0.0 copy-start.2
  9.7 1.1 %pad_maximum_fusion.held = f32[2,384,128]{2,1,0:T(8,128)S(1)} fusion(f32[2,128,128]{2,1,0:T(8,128)} %constant.66.clone, f32[2,256,128]{2,1,0:T(8,128)} %bitcast.28), kind=kLoop, calls=%fused_computation.1 | loop fusion | flops 98304 | bytes 786432 | tf_op jit(solution)/shard_map/concatenate | solution.py:242
  10.8 0.0 collective-permute-done.below
  10.8 0.0 collective-permute-done.1.right
  10.8 0.0 collective-permute-done.2.other_diag
  10.8 0.3 collective-permute-done.3.diag
  11.1 0.0 collective-permute-done.4.other_below
  11.1 0.0 copy-done
  11.1 0.0 copy-done.1
  11.1 0.0 copy-done.2
  11.1 5.1 %shard_map.77 = (f32[2,128,128]{2,1,0:T(8,128)S(1)}, f32[2,128,128]{2,1,0:T(8,128)S(1)}, f32[2,2,128,128]{3,2,1,0:T(8,128)S(1)}, f32[4,128,128]{2,1,0:T(8,128)S(1)}, f32[4,128,128]{2,1,0:T(8,128)S(1)}) custom-call(s32[1,2,4]{2,1,0:T(2,128)S(1)} %copy-done.2, s32[1,1]{1,0:T(1,128)S(6)} %copy.8.counts, s32[5]{0:T(128)S(1)} %stack.31.place, ...), custom_call_target="tpu_custom_call" | custom-call | tf_op jit(solution)/shard_map/pallas_call | solution.py:252
  16.2 0.1 collective-permute-start.5
  16.3 2.3 %collective-permute-start.7 = (f32[2,2,128,128]{3,2,1,0:T(8,128)S(1)}, f32[2,2,128,128]{3,2,1,0:T(8,128)S(1)}, u32[]{:S(2)}, u32[]{:S(2)}) collective-permute-start(f32[2,2,128,128]{3,2,1,0:T(8,128)S(1)} %get-tuple-element.18), channel_id=1, source_target_pairs={{0,8},{1,9},{2,10},{3,11},{4,12},{5,13},{6,14},{7,15},{8,16},{9,17... | collective-permute-start | bytes 786440 | tf_op jit(solution)/shard_map/ppermute | solution.py:207
  18.6 0.0 collective-permute-done.5
  18.6 2.3 %collective-permute-start.6 = (f32[128,128]{1,0:T(8,128)S(1)}, f32[128,128]{1,0:T(8,128)S(1)}, u32[]{:S(2)}, u32[]{:S(2)}) collective-permute-start(f32[128,128]{1,0:T(8,128)S(1)} %get-tuple-element.30), channel_id=1, source_target_pairs={{0,6},{1,7},{2,4},{3,5},{4,2},{5,3},{6,0},{7,1},{8,14},{9,15},{10,... | collective-permute-start | bytes 196616 | tf_op jit(solution)/shard_map/ppermute | solution.py:212
  20.9 0.0 collective-permute-start.8
  20.9 1.3 %collective-permute-start.9 = (f32[128,128]{1,0:T(8,128)S(1)}, f32[128,128]{1,0:T(8,128)S(1)}, u32[]{:S(2)}, u32[]{:S(2)}) collective-permute-start(f32[128,128]{1,0:T(8,128)S(1)} %get-tuple-element.29), channel_id=1, source_target_pairs={{0,4},{1,5},{2,6},{3,7},{4,0},{5,1},{6,2},{7,3},{8,12},{9,13},{10,... | collective-permute-start | bytes 196616 | tf_op jit(solution)/shard_map/ppermute | solution.py:212
  22.2 4.6 %collective-permute-done.7 = f32[2,2,128,128]{3,2,1,0:T(8,128)S(1)} collective-permute-done((f32[2,2,128,128]{3,2,1,0:T(8,128)S(1)}, f32[2,2,128,128]{3,2,1,0:T(8,128)S(1)}, u32[]{:S(2)}, u32[]{:S(2)}) %collective-permute-start.7) | collective-permute-done | bytes 262176 | tf_op jit(solution)/shard_map/ppermute | solution.py:207
  26.8 0.0 collective-permute-done.6
  26.8 0.0 collective-permute-done.8
  26.8 0.0 collective-permute-done.9
  26.8 0.5 %collective-permute-start.10 = (f32[128,128]{1,0:T(8,128)S(1)}, f32[128,128]{1,0:T(8,128)S(1)}, u32[]{:S(2)}, u32[]{:S(2)}) collective-permute-start(f32[128,128]{1,0:T(8,128)S(1)} %fusion.3), channel_id=1, source_target_pairs={{0,8},{1,9},{2,10},{3,11},{4,12},{5,13},{6,14},{7,15},{8,0},{9,1},... | collective-permute-start | bytes 196616 | tf_op jit(solution)/shard_map/ppermute | solution.py:212
  27.3 1.1 %collective-permute-start.11 = (f32[128,128]{1,0:T(8,128)S(1)}, f32[128,128]{1,0:T(8,128)S(1)}, u32[]{:S(2)}, u32[]{:S(2)}) collective-permute-start(f32[128,128]{1,0:T(8,128)S(1)} %fusion.3), channel_id=1, source_target_pairs={{0,16},{1,17},{2,18},{3,19},{4,20},{5,21},{6,22},{7,23},{8,24},{9,... | collective-permute-start | bytes 196616 | tf_op jit(solution)/shard_map/ppermute | solution.py:212
  28.4 2.9 %collective-permute-start.12 = (f32[128,128]{1,0:T(8,128)S(1)}, f32[128,128]{1,0:T(8,128)S(1)}, u32[]{:S(2)}, u32[]{:S(2)}) collective-permute-start(f32[128,128]{1,0:T(8,128)S(1)} %fusion.3), channel_id=1, source_target_pairs={{0,24},{1,25},{2,26},{3,27},{4,28},{5,29},{6,30},{7,31},{8,16},{9,... | collective-permute-start | bytes 196616 | tf_op jit(solution)/shard_map/ppermute | solution.py:212
  31.3 0.1 collective-permute-start.14
  31.3 0.2 collective-permute-done.10
  31.6 3.9 %collective-permute-done.11 = f32[128,128]{1,0:T(8,128)S(1)} collective-permute-done((f32[128,128]{1,0:T(8,128)S(1)}, f32[128,128]{1,0:T(8,128)S(1)}, u32[]{:S(2)}, u32[]{:S(2)}) %collective-permute-start.11) | collective-permute-done | bytes 65568 | tf_op jit(solution)/shard_map/ppermute | solution.py:212
  35.5 0.0 collective-permute-done.12
  35.5 1.2 %collective-permute-start.13 = (f32[128,128]{1,0:T(8,128)S(1)}, f32[128,128]{1,0:T(8,128)S(1)}, u32[]{:S(2)}, u32[]{:S(2)}) collective-permute-start(f32[128,128]{1,0:T(8,128)S(1)} %add_add_fusion), channel_id=1, source_target_pairs={{0,6},{1,7},{2,4},{3,5},{4,2},{5,3},{6,0},{7,1},{8,14},{9,15},{10,... | collective-permute-start | bytes 196616 | tf_op jit(solution)/shard_map/ppermute | solution.py:212
  36.7 0.6 %collective-permute-start.19 = (f32[128,128]{1,0:T(8,128)S(1)}, f32[128,128]{1,0:T(8,128)S(1)}, u32[]{:S(2)}, u32[]{:S(2)}) collective-permute-start(f32[128,128]{1,0:T(8,128)S(1)} %add_add_fusion), channel_id=1, source_target_pairs={{0,4},{1,5},{2,6},{3,7},{4,0},{5,1},{6,2},{7,3},{8,12},{9,13},{10,... | collective-permute-start | bytes 196616 | tf_op jit(solution)/shard_map/ppermute | solution.py:212
  37.3 1.7 %collective-permute-start.15 = (f32[128,128]{1,0:T(8,128)S(1)}, f32[128,128]{1,0:T(8,128)S(1)}, u32[]{:S(2)}, u32[]{:S(2)}) collective-permute-start(f32[128,128]{1,0:T(8,128)S(1)} %add_add_fusion), channel_id=1, source_target_pairs={{0,2},{1,3},{2,0},{3,1},{4,6},{5,7},{6,4},{7,5},{8,10},{9,11},{10,... | collective-permute-start | bytes 196616 | tf_op jit(solution)/shard_map/ppermute | solution.py:212
  39.0 0.0 collective-permute-start.17
  39.0 1.7 %collective-permute-done.13 = f32[128,128]{1,0:T(8,128)S(1)} collective-permute-done((f32[128,128]{1,0:T(8,128)S(1)}, f32[128,128]{1,0:T(8,128)S(1)}, u32[]{:S(2)}, u32[]{:S(2)}) %collective-permute-start.13) | collective-permute-done | bytes 65568 | tf_op jit(solution)/shard_map/ppermute | solution.py:212
  40.8 0.0 collective-permute-done.14
  40.8 0.0 collective-permute-start.18
  40.8 0.7 %fusion = f32[2,128,128]{2,1,0:T(8,128)} fusion(f32[2,128,128]{2,1,0:T(8,128)S(1)} %collective-permute-done.14, f32[2,128,128]{2,1,0:T(8,128)S(1)} %get-tuple-element.15, f32[2,2,128,128]{3,2,1,0:T(8,128)S(1)} %collective-permute-done.7), kind=kLoop, calls=%fused_computation.10 | loop fusion | flops 65536 | bytes 524288 | tf_op jit(solution)/shard_map/add | solution.py:281
  41.4 0.0 collective-permute-done.19
  41.4 0.5 %collective-permute-start.20 = (f32[128,128]{1,0:T(8,128)S(1)}, f32[128,128]{1,0:T(8,128)S(1)}, u32[]{:S(2)}, u32[]{:S(2)}) collective-permute-start(f32[128,128]{1,0:T(8,128)S(1)} %collective-permute-done.19), channel_id=1, source_target_pairs={{0,1},{1,0},{2,3},{3,2},{4,5},{5,4},{6,7},{7,6},{8,9},{9,8},{10,11... | collective-permute-start | bytes 196616 | tf_op jit(solution)/shard_map/ppermute | solution.py:212
  42.0 0.0 collective-permute-done.15
  42.0 0.1 collective-permute-start.16
  42.1 0.0 collective-permute-done.18
  42.1 0.8 %collective-permute-done.20 = f32[128,128]{1,0:T(8,128)S(1)} collective-permute-done((f32[128,128]{1,0:T(8,128)S(1)}, f32[128,128]{1,0:T(8,128)S(1)}, u32[]{:S(2)}, u32[]{:S(2)}) %collective-permute-start.20) | collective-permute-done | bytes 65568 | tf_op jit(solution)/shard_map/ppermute | solution.py:212
  42.9 0.0 collective-permute-done.17
  42.9 0.4 collective-permute-done.16
  43.4 0.8 %maximum_select_fusion = f32[1024,128]{1,0:T(8,128)} fusion(f32[512,128]{1,0:T(8,128)S(1)} %get-tuple-element.32, f32[512,128]{1,0:T(8,128)S(1)} %get-tuple-element.31, pred[]{:T(512)S(6)} %eq.18), kind=kLoop, calls=%fused_computation | loop fusion | flops 393216 | bytes 1048577 | tf_op jit(solution)/shard_map/jit(_where)/select_n | solution.py:287
  (10 shorter events, 0.2 us)
Async XLA Ops:
  0.6 10.5 %copy-start = (f32[2,4,128,128]{3,2,1,0:T(8,128)S(1)}, f32[2,4,128,128]{3,2,1,0:T(8,128)}, u32[]{:S(2)}) copy-start(f32[2,4,128,128]{3,2,1,0:T(8,128)} %probes.1) | copy-start | bytes 1572868
  0.6 10.2 %collective-permute-start = (bf16[2,128,128]{2,1,0:T(8,128)(2,1)}, bf16[2,128,128]{2,1,0:T(8,128)(2,1)S(1)}, u32[]{:S(2)}, u32[]{:S(2)}) collective-permute-start(bf16[2,128,128]{2,1,0:T(8,128)(2,1)} %own.1), channel_id=1, source_target_pairs={{0,8},{1,9},{2,10},{3,11},{4,12},{5,13},{6,14},{7,15},{8,0},{9,1},... | collective-permute-start | bytes 196616 | tf_op jit(solution)/shard_map/ppermute | solution.py:234
  3.7 7.1 %collective-permute-start.1 = (bf16[2,128,128]{2,1,0:T(8,128)(2,1)}, bf16[2,128,128]{2,1,0:T(8,128)(2,1)S(1)}, u32[]{:S(2)}, u32[]{:S(2)}) collective-permute-start(bf16[2,128,128]{2,1,0:T(8,128)(2,1)} %own.1), channel_id=1, source_target_pairs={{0,7},{1,0},{2,1},{3,2},{4,3},{5,4},{6,5},{7,6},{8,15},{9,8},{10,9... | collective-permute-start | bytes 196616 | tf_op jit(solution)/shard_map/ppermute | solution.py:207
  5.3 5.5 %collective-permute-start.2 = (bf16[2,128,128]{2,1,0:T(8,128)(2,1)}, bf16[2,128,128]{2,1,0:T(8,128)(2,1)S(1)}, u32[]{:S(2)}, u32[]{:S(2)}) collective-permute-start(bf16[2,128,128]{2,1,0:T(8,128)(2,1)} %own.1), channel_id=1, source_target_pairs={{0,7},{1,0},{2,1},{3,2},{4,3},{5,4},{6,5},{7,6},{8,23},{9,16},{10,... | collective-permute-start | bytes 196616 | tf_op jit(solution)/shard_map/ppermute | solution.py:234
  6.3 4.8 %collective-permute-start.3 = (bf16[2,128,128]{2,1,0:T(8,128)(2,1)}, bf16[2,128,128]{2,1,0:T(8,128)(2,1)S(1)}, u32[]{:S(2)}, u32[]{:S(2)}) collective-permute-start(bf16[2,128,128]{2,1,0:T(8,128)(2,1)} %own.1), channel_id=1, source_target_pairs={{0,15},{1,8},{2,9},{3,10},{4,11},{5,12},{6,13},{7,14},{8,7},{9,0},... | collective-permute-start | bytes 196616 | tf_op jit(solution)/shard_map/ppermute | solution.py:234
  8.5 2.6 %collective-permute-start.4 = (bf16[2,128,128]{2,1,0:T(8,128)(2,1)}, bf16[2,128,128]{2,1,0:T(8,128)(2,1)S(1)}, u32[]{:S(2)}, u32[]{:S(2)}) collective-permute-start(bf16[2,128,128]{2,1,0:T(8,128)(2,1)} %own.1), channel_id=1, source_target_pairs={{0,1},{1,0},{2,3},{3,2},{4,5},{5,4},{6,7},{7,6},{8,16},{9,17},{10,... | collective-permute-start | bytes 196616 | tf_op jit(solution)/shard_map/ppermute | solution.py:234
  9.7 1.4 %copy-start.1 = (bf16[2,128,128]{2,1,0:T(8,128)(2,1)S(1)}, bf16[2,128,128]{2,1,0:T(8,128)(2,1)}, u32[]{:S(2)}) copy-start(bf16[2,128,128]{2,1,0:T(8,128)(2,1)} %own.1) | copy-start | bytes 196612
  9.7 1.4 %copy-start.2 = (s32[1,2,4]{2,1,0:T(2,128)S(1)}, s32[1,2,4]{2,1,0:T(2,128)}, u32[]{:S(2)}) copy-start(s32[1,2,4]{2,1,0:T(2,128)} %offsets.1) | copy-start | bytes 100
  16.2 2.4 %collective-permute-start.5 = (f32[4,128,128]{2,1,0:T(8,128)S(1)}, f32[4,128,128]{2,1,0:T(8,128)S(1)}, u32[]{:S(2)}, u32[]{:S(2)}) collective-permute-start(f32[4,128,128]{2,1,0:T(8,128)S(1)} %get-tuple-element.17), channel_id=1, source_target_pairs={{0,1},{1,0},{2,3},{3,2},{4,5},{5,4},{6,7},{7,6},{8,9},{9,8},{10,11... | collective-permute-start | bytes 786440 | tf_op jit(solution)/shard_map/ppermute | solution.py:212
  16.3 10.5 %collective-permute-start.7 = (f32[2,2,128,128]{3,2,1,0:T(8,128)S(1)}, f32[2,2,128,128]{3,2,1,0:T(8,128)S(1)}, u32[]{:S(2)}, u32[]{:S(2)}) collective-permute-start(f32[2,2,128,128]{3,2,1,0:T(8,128)S(1)} %get-tuple-element.18), channel_id=1, source_target_pairs={{0,8},{1,9},{2,10},{3,11},{4,12},{5,13},{6,14},{7,15},{8,16},{9,17... | collective-permute-start | bytes 786440 | tf_op jit(solution)/shard_map/ppermute | solution.py:207
  18.6 8.1 %collective-permute-start.6 = (f32[128,128]{1,0:T(8,128)S(1)}, f32[128,128]{1,0:T(8,128)S(1)}, u32[]{:S(2)}, u32[]{:S(2)}) collective-permute-start(f32[128,128]{1,0:T(8,128)S(1)} %get-tuple-element.30), channel_id=1, source_target_pairs={{0,6},{1,7},{2,4},{3,5},{4,2},{5,3},{6,0},{7,1},{8,14},{9,15},{10,... | collective-permute-start | bytes 196616 | tf_op jit(solution)/shard_map/ppermute | solution.py:212
  20.9 5.9 %collective-permute-start.8 = (f32[128,128]{1,0:T(8,128)S(1)}, f32[128,128]{1,0:T(8,128)S(1)}, u32[]{:S(2)}, u32[]{:S(2)}) collective-permute-start(f32[128,128]{1,0:T(8,128)S(1)} %get-tuple-element.28), channel_id=1, source_target_pairs={{0,2},{1,3},{2,0},{3,1},{4,6},{5,7},{6,4},{7,5},{8,10},{9,11},{10,... | collective-permute-start | bytes 196616 | tf_op jit(solution)/shard_map/ppermute | solution.py:212
  20.9 5.9 %collective-permute-start.9 = (f32[128,128]{1,0:T(8,128)S(1)}, f32[128,128]{1,0:T(8,128)S(1)}, u32[]{:S(2)}, u32[]{:S(2)}) collective-permute-start(f32[128,128]{1,0:T(8,128)S(1)} %get-tuple-element.29), channel_id=1, source_target_pairs={{0,4},{1,5},{2,6},{3,7},{4,0},{5,1},{6,2},{7,3},{8,12},{9,13},{10,... | collective-permute-start | bytes 196616 | tf_op jit(solution)/shard_map/ppermute | solution.py:212
  26.8 4.8 %collective-permute-start.10 = (f32[128,128]{1,0:T(8,128)S(1)}, f32[128,128]{1,0:T(8,128)S(1)}, u32[]{:S(2)}, u32[]{:S(2)}) collective-permute-start(f32[128,128]{1,0:T(8,128)S(1)} %fusion.3), channel_id=1, source_target_pairs={{0,8},{1,9},{2,10},{3,11},{4,12},{5,13},{6,14},{7,15},{8,0},{9,1},... | collective-permute-start | bytes 196616 | tf_op jit(solution)/shard_map/ppermute | solution.py:212
  27.3 8.1 %collective-permute-start.11 = (f32[128,128]{1,0:T(8,128)S(1)}, f32[128,128]{1,0:T(8,128)S(1)}, u32[]{:S(2)}, u32[]{:S(2)}) collective-permute-start(f32[128,128]{1,0:T(8,128)S(1)} %fusion.3), channel_id=1, source_target_pairs={{0,16},{1,17},{2,18},{3,19},{4,20},{5,21},{6,22},{7,23},{8,24},{9,... | collective-permute-start | bytes 196616 | tf_op jit(solution)/shard_map/ppermute | solution.py:212
  28.4 7.1 %collective-permute-start.12 = (f32[128,128]{1,0:T(8,128)S(1)}, f32[128,128]{1,0:T(8,128)S(1)}, u32[]{:S(2)}, u32[]{:S(2)}) collective-permute-start(f32[128,128]{1,0:T(8,128)S(1)} %fusion.3), channel_id=1, source_target_pairs={{0,24},{1,25},{2,26},{3,27},{4,28},{5,29},{6,30},{7,31},{8,16},{9,... | collective-permute-start | bytes 196616 | tf_op jit(solution)/shard_map/ppermute | solution.py:212
  31.3 9.5 %collective-permute-start.14 = (f32[2,128,128]{2,1,0:T(8,128)S(1)}, f32[2,128,128]{2,1,0:T(8,128)S(1)}, u32[]{:S(2)}, u32[]{:S(2)}) collective-permute-start(f32[2,128,128]{2,1,0:T(8,128)S(1)} %bitcast_add_fusion), channel_id=1, source_target_pairs={{0,1},{1,2},{2,3},{3,4},{4,5},{5,6},{6,7},{7,0},{8,9},{9,10},{10,1... | collective-permute-start | bytes 393224 | tf_op jit(solution)/shard_map/ppermute | solution.py:207
  35.5 5.3 %collective-permute-start.13 = (f32[128,128]{1,0:T(8,128)S(1)}, f32[128,128]{1,0:T(8,128)S(1)}, u32[]{:S(2)}, u32[]{:S(2)}) collective-permute-start(f32[128,128]{1,0:T(8,128)S(1)} %add_add_fusion), channel_id=1, source_target_pairs={{0,6},{1,7},{2,4},{3,5},{4,2},{5,3},{6,0},{7,1},{8,14},{9,15},{10,... | collective-permute-start | bytes 196616 | tf_op jit(solution)/shard_map/ppermute | solution.py:212
  36.7 4.7 %collective-permute-start.19 = (f32[128,128]{1,0:T(8,128)S(1)}, f32[128,128]{1,0:T(8,128)S(1)}, u32[]{:S(2)}, u32[]{:S(2)}) collective-permute-start(f32[128,128]{1,0:T(8,128)S(1)} %add_add_fusion), channel_id=1, source_target_pairs={{0,4},{1,5},{2,6},{3,7},{4,0},{5,1},{6,2},{7,3},{8,12},{9,13},{10,... | collective-permute-start | bytes 196616 | tf_op jit(solution)/shard_map/ppermute | solution.py:212
  37.3 4.7 %collective-permute-start.15 = (f32[128,128]{1,0:T(8,128)S(1)}, f32[128,128]{1,0:T(8,128)S(1)}, u32[]{:S(2)}, u32[]{:S(2)}) collective-permute-start(f32[128,128]{1,0:T(8,128)S(1)} %add_add_fusion), channel_id=1, source_target_pairs={{0,2},{1,3},{2,0},{3,1},{4,6},{5,7},{6,4},{7,5},{8,10},{9,11},{10,... | collective-permute-start | bytes 196616 | tf_op jit(solution)/shard_map/ppermute | solution.py:212
  39.0 3.8 %collective-permute-start.17 = (f32[128,128]{1,0:T(8,128)S(1)}, f32[128,128]{1,0:T(8,128)S(1)}, u32[]{:S(2)}, u32[]{:S(2)}) collective-permute-start(f32[128,128]{1,0:T(8,128)S(1)} %add_add_fusion), channel_id=1, source_target_pairs={{0,1},{1,0},{2,3},{3,2},{4,5},{5,4},{6,7},{7,6},{8,9},{9,8},{10,11... | collective-permute-start | bytes 196616 | tf_op jit(solution)/shard_map/ppermute | solution.py:212
  40.8 1.3 %collective-permute-start.18 = (f32[128,128]{1,0:T(8,128)S(1)}, f32[128,128]{1,0:T(8,128)S(1)}, u32[]{:S(2)}, u32[]{:S(2)}) collective-permute-start(f32[128,128]{1,0:T(8,128)S(1)} %collective-permute-done.13), channel_id=1, source_target_pairs={{0,1},{1,0},{2,3},{3,2},{4,5},{5,4},{6,7},{7,6},{8,9},{9,8},{10,11... | collective-permute-start | bytes 196616 | tf_op jit(solution)/shard_map/ppermute | solution.py:212
  41.4 1.4 %collective-permute-start.20 = (f32[128,128]{1,0:T(8,128)S(1)}, f32[128,128]{1,0:T(8,128)S(1)}, u32[]{:S(2)}, u32[]{:S(2)}) collective-permute-start(f32[128,128]{1,0:T(8,128)S(1)} %collective-permute-done.19), channel_id=1, source_target_pairs={{0,1},{1,0},{2,3},{3,2},{4,5},{5,4},{6,7},{7,6},{8,9},{9,8},{10,11... | collective-permute-start | bytes 196616 | tf_op jit(solution)/shard_map/ppermute | solution.py:212
  42.0 1.3 %collective-permute-start.16 = (f32[128,128]{1,0:T(8,128)S(1)}, f32[128,128]{1,0:T(8,128)S(1)}, u32[]{:S(2)}, u32[]{:S(2)}) collective-permute-start(f32[128,128]{1,0:T(8,128)S(1)} %collective-permute-done.15), channel_id=1, source_target_pairs={{0,1},{1,0},{2,3},{3,2},{4,5},{5,4},{6,7},{7,6},{8,9},{9,8},{10,11... | collective-permute-start | bytes 196616 | tf_op jit(solution)/shard_map/ppermute | solution.py:212
